TPU v7x, 32 devices: a whole 2x2x4 slice. The times are simulated.
32 devices in a mesh: group: 2 (over x), replica: 4 (over y, core), tensor: 4 (over z).
Axes of the slice: x: 2, y: 2, z: 4, core: 2. Of those that a mesh axis runs over, the one named last changes fastest.
Arguments:
- hidden_state_rows: bfloat16 [64, 8192], P(('group', 'replica'), 'tensor'), parts along dimension 0, may hold values from -6 to 6
- queries: bfloat16 [64, 64, 128], P(('group', 'replica'), 'tensor'), parts along dimension 0, may hold values from -150 to 150
- rotated_key_cache: bfloat16 [64, 8, 1024, 128], P(('group', 'replica'), 'tensor'), parts along dimension 0, may hold values from -6 to 6
- cached_value_rows: bfloat16 [64, 8, 1024, 128], P(('group', 'replica'), 'tensor'), parts along dimension 0, may hold values from -6 to 6
- lengths: int32 [64], P(('group', 'replica')), parts along dimension 0, may hold values from 2 to 1024, as said below
- row_adapter_index: int32 [64], P(('group', 'replica')), parts along dimension 0, may hold values from 0 to 63
- key_value_weight: bfloat16 [8192, 2, 1024], P(None, None, 'tensor'), may hold values from -0.0625 to 0.0625
- adapter_down_weight: bfloat16 [128, 8192, 32], P(('group', 'replica'), 'tensor'), parts along dimension 0, may hold values from -0.0625 to 0.0625
- adapter_up_weight: bfloat16 [128, 2, 16, 1024], P(('group', 'replica'), None, None, 'tensor'), parts along dimension 0, may hold values from -1.5 to 1.5
Outputs:
- attention: bfloat16 [64, 8192], P(('group', 'replica'), 'tensor'), parts along dimension 0
There are 2 independent parts, one for each index of `group`. A program takes and returns all parts, laid end to end along the dimension named above; an argument that names none is the same for every part. Nothing has to cross between parts.
Inputs may be any that keep to these rules, and one draw needn't show every extreme that they name: `lengths`: the first of each 8 consecutive rows has all 1024 positions in use.
All inputs are finite; a program needn't handle non-finite values.
Results may differ from a plain program's by a relative error of at most 0.009.
Values may be sent and summed in bfloat16 or wider, within the bound.
A program may use at most 128 MiB of HBM per device.

v0:
```python
import math

import jax
import jax.numpy as jnp
from jax import lax
from jax.sharding import PartitionSpec as P

adapter_scale = 2.0


def rotate_keys(vectors, positions):
    head_width = vectors.shape[-1]
    half_size = head_width // 2
    frequency = jnp.exp(
        jnp.arange(half_size, dtype=jnp.float32) * (-2.0 * math.log(500000.0) / head_width)
    )
    angles = positions.astype(jnp.float32)[:, None] * frequency[None, :]
    cosine = jnp.cos(angles)[:, None, :]
    sine = jnp.sin(angles)[:, None, :]
    front_part = vectors[..., :half_size]
    back_part = vectors[..., half_size:]
    return jnp.concatenate(
        [front_part * cosine - back_part * sine, back_part * cosine + front_part * sine], axis=-1
    )


def on_device(
    hidden_state_rows,
    queries,
    rotated_key_cache,
    cached_value_rows,
    lengths,
    row_adapter_index,
    key_value_weight,
    adapter_down_weight,
    adapter_up_weight,
):
    request_row_count = hidden_state_rows.shape[0]
    shard_heads = rotated_key_cache.shape[1]
    head_width = rotated_key_cache.shape[3]
    kv_width = shard_heads * head_width
    weight_flat = key_value_weight.reshape(key_value_weight.shape[0], 2 * kv_width)
    rank_width = adapter_down_weight.shape[2] // 2
    base_projection = jnp.dot(
        lax.all_gather(hidden_state_rows, "tensor", axis=1, tiled=True),
        weight_flat,
        preferred_element_type=jnp.float32,
    )
    every_in, every_out = (
        lax.all_gather(adapter_down_weight, "replica", axis=0, tiled=True),
        lax.all_gather(adapter_up_weight, "replica", axis=0, tiled=True),
    )
    picked_in = jnp.take(every_in, row_adapter_index, axis=0)
    partial_low = jnp.einsum(
        "rd,rdk->rk", hidden_state_rows, picked_in, preferred_element_type=jnp.float32
    )
    reduced_rank_state = lax.psum(partial_low, "tensor")
    picked_out = jnp.take(every_out, row_adapter_index, axis=0).astype(jnp.float32)
    adapter_update = jnp.einsum(
        "rpj,rpjk->rpk",
        reduced_rank_state.reshape(request_row_count, 2, rank_width),
        picked_out,
        precision=lax.Precision.HIGHEST,
    ).reshape(request_row_count, 2 * kv_width)
    projected_rows = (base_projection + adapter_scale * adapter_update).reshape(
        request_row_count, 2, shard_heads, head_width
    )
    new_key = rotate_keys(projected_rows[:, 0], lengths).astype(jnp.bfloat16)
    new_value = projected_rows[:, 1].astype(jnp.bfloat16)
    group_size = queries.shape[1] // shard_heads
    score_scale = head_width ** (-0.5)
    grouped = queries.reshape(request_row_count, shard_heads, group_size, head_width)
    cache_length = rotated_key_cache.shape[2]
    scores = (
        jnp.einsum(
            "rkgd,rktd->rkgt", grouped, rotated_key_cache, preferred_element_type=jnp.float32
        )
        * score_scale
    )
    visible = jnp.arange(cache_length, dtype=jnp.int32)[None, :] < lengths[:, None]
    scores = jnp.where(visible[:, None, None, :], scores, -1e30)
    fresh_score = (
        jnp.einsum("rkgd,rkd->rkg", grouped, new_key, preferred_element_type=jnp.float32)
        * score_scale
    )
    peak_score = jnp.maximum(jnp.max(scores, axis=-1), fresh_score)
    weights_raw = jnp.exp(scores - peak_score[..., None])
    fresh_raw = jnp.exp(fresh_score - peak_score)
    denominator = jnp.sum(weights_raw, axis=-1) + fresh_raw
    weights = (weights_raw / denominator[..., None]).astype(jnp.bfloat16)
    fresh_weight = (fresh_raw / denominator).astype(jnp.bfloat16)
    mixed = jnp.einsum(
        "rkgt,rktd->rkgd", weights, cached_value_rows, preferred_element_type=jnp.float32
    )
    mixed = (
        mixed
        + fresh_weight.astype(jnp.float32)[..., None] * new_value.astype(jnp.float32)[:, :, None, :]
    )
    return mixed.reshape(request_row_count, shard_heads * group_size * head_width).astype(
        jnp.bfloat16
    )


def solution(mesh):
    in_specs = (
        P(("group", "replica"), "tensor"),
        P(("group", "replica"), "tensor", None),
        P(("group", "replica"), "tensor", None, None),
        P(("group", "replica"), "tensor", None, None),
        P(("group", "replica")),
        P(("group", "replica")),
        P(None, None, "tensor"),
        P(("group", "replica"), "tensor", None),
        P(("group", "replica"), None, None, "tensor"),
    )
    out_specs = P(("group", "replica"), "tensor")
    return jax.shard_map(
        on_device, mesh=mesh, in_specs=in_specs, out_specs=out_specs, check_vma=False
    )
```

profile of v0, /device:TPU:0, one launch (start us, length us, event | category | flops | bytes accessed | tf_op | source)
XLA Modules:
  0.0 118.5 jit_solution(6936530249804305128)
XLA Ops:
  6.5 0.0 copy-start
  6.5 0.0 all-gather.5.cloned.1.call-start
  6.5 0.7 all-gather.5.cloned.1.call-update
  7.3 0.0 all-gather.3.cloned.1.call-start
  7.3 0.7 all-gather.3.cloned.1.call-update
  8.0 0.0 copy-start.3
  8.0 0.0 copy-start.2
  8.0 0.0 copy-start.5
  8.0 0.0 copy-start.1
  8.0 8.2 %copy.18 = bf16[1024,8,2,256]{3,1,2,0:T(8,128)(2,1)} copy(bf16[1024,8,2,256]{3,2,1,0:T(2,128)(2,1)} %bitcast.42) | data formatting | bytes 16777216
  16.3 0.0 copy-done.3
  16.3 0.0 copy-done.2
  16.3 15.1 %all_gather.9 = bf16[8,8192]{1,0:T(8,128)(2,1)S(1)} all-gather(bf16[8,2048]{1,0:T(8,128)(2,1)S(1)} %copy-done.2), channel_id=1, replica_groups=mesh['group'=2,'replica'=4,'tensor'=4] {'tensor'}, dimensions={1}, use_global_device_ids=true | all-gather | bytes 163840 | tf_op jit(solution)/shard_map/all_gather | solution.py:45
  31.3 0.0 copy-done.5
  31.4 0.1 iota_compare_fusion
  31.4 0.1 multiply_cosine_fusion
  31.6 0.0 copy-done
  31.6 0.0 copy-done.1
  31.6 1.3 %fusion.25 = (f32[8,2,8]{2,1,0:T(2,128)S(1)}, f32[8,2,8,1024]{3,2,1,0:T(8,128)S(1)}) fusion(bf16[8,2,1024,128]{3,2,1,0:T(8,128)(2,1)S(1)} %copy-done.1, bf16[8,16,128]{2,1,0:T(8,128)(2,1)S(1)} %copy-done, pred[8,1024]{1,0:T(8,128)(4,1)S(1)} %iota_compare_fusion), kind=kOutput, calls=%fused_computation.49 | convolution fusion | flops 33947520 | bytes 4760064 | tf_op jit(solution)/shard_map/rkgd,rktd->rkgt/dot_general | solution.py:75
  32.9 0.0 all-gather.5.cloned.1.call-done
  32.9 1.8 %gather_fusion.1 = bf16[8,2,16,256]{3,2,1,0:T(8,128)(2,1)S(1)} fusion(bf16[64,2,16,256]{3,2,1,0:T(8,128)(2,1)} %all-gather.5.cloned.1.call-done, s32[1024]{0:T(1024)S(1)} %pad_clamp_fusion), kind=kCustom, calls=%fused_computation.1 | custom fusion | bytes 262176 | tf_op jit(solution)/shard_map/jit(_take)/gather | solution.py:58
  34.7 53.6 %all-gather.3.cloned.1.call-done = bf16[64,2048,32]{1,2,0:T(8,128)(2,1)} async-done(((bf16[16,2048,32]{1,2,0:T(8,128)(2,1)}), bf16[64,2048,32]{1,2,0:T(8,128)(2,1)}) %all-gather.3.cloned.1.call-update) | async-done | bytes 8388624 | tf_op jit(solution)/shard_map/all_gather | solution.py:50
  88.3 4.0 %gather_fusion = bf16[8,2048,32]{1,2,0:T(8,128)(2,1)S(1)} fusion(bf16[64,2048,32]{1,2,0:T(8,128)(2,1)} %all-gather.3.cloned.1.call-done, s32[1024]{0:T(1024)S(1)} %pad_clamp_fusion), kind=kCustom, calls=%fused_computation | custom fusion | bytes 2097184 | tf_op jit(solution)/shard_map/jit(_take)/gather | solution.py:53
  92.3 0.4 fusion.3
  92.7 0.1 reshape.103
  92.8 11.8 %psum.7 = f32[8,2,16]{2,1,0:T(2,128)S(1)} all-reduce(f32[8,2,16]{2,1,0:T(2,128)S(1)} %reshape.103), channel_id=1, replica_groups=mesh['group'=2,'replica'=4,'tensor'=4] {'tensor'}, use_global_device_ids=true, to_apply=%region_1.2 | all-reduce | flops 256 | bytes 2048 | tf_op jit(solution)/shard_map/psum | solution.py:57
  104.6 0.3 fusion.10
  104.9 0.0 copy-start.4
  104.9 4.7 %convolution_add_fusion.1 = f32[8,512]{1,0:T(8,128)S(1)} fusion(f32[8,512]{1,0:T(8,128)S(1)} %bitcast.43, bf16[8,8192]{1,0:T(8,128)(2,1)S(1)} %all_gather.9, bf16[8192,512]{1,0:T(8,128)(2,1)} %bitcast.41), kind=kOutput, calls=%fused_computation.7 | convolution fusion | flops 67112960 | bytes 8552448 | tf_op jit(solution)/shard_map/dot_general | solution.py:44
  109.6 0.1 subtract_convert_fusion
  109.7 0.1 maximum_bitcast_fusion
  109.8 0.1 fusion.15
  110.0 0.2 fusion.7
  110.3 0.0 copy-done.4
  110.3 0.7 fusion.2
  111.0 0.6 copy.26
  (11 shorter events, 0.1 us)
Async XLA Ops:
  6.5 25.0 %copy-start = (bf16[8,16,128]{2,1,0:T(8,128)(2,1)S(1)}, bf16[8,16,128]{2,1,0:T(8,128)(2,1)}, u32[]{:S(2)}) copy-start(bf16[8,16,128]{2,1,0:T(8,128)(2,1)} %param.10) | copy-start | bytes 98308
  6.5 26.3 %all-gather.5.cloned.1.call-start = ((), (), s32[]{:S(2)}) async-start(), calls=%async_computation.1 | async-start | bytes 1310720 | tf_op jit(solution)/shard_map/all_gather | solution.py:51
  7.3 81.0 %all-gather.3.cloned.1.call-start = ((), (), s32[]{:S(2)}) async-start(), calls=%async_computation | async-start | bytes 10485760 | tf_op jit(solution)/shard_map/all_gather | solution.py:50
  8.0 8.2 %copy-start.3 = (s32[8]{0:T(128)S(1)}, s32[8]{0:T(128)}, u32[]{:S(2)}) copy-start(s32[8]{0:T(128)} %param.13) | copy-start | bytes 100
  8.0 8.2 %copy-start.2 = (bf16[8,2048]{1,0:T(8,128)(2,1)S(1)}, bf16[8,2048]{1,0:T(8,128)(2,1)}, u32[]{:S(2)}) copy-start(bf16[8,2048]{1,0:T(8,128)(2,1)} %param.9) | copy-start | bytes 98308
  8.0 23.3 %copy-start.5 = (s32[8]{0:T(128)S(1)}, s32[8]{0:T(128)}, u32[]{:S(2)}) copy-start(s32[8]{0:T(128)} %param.14) | copy-start | bytes 100
  8.0 23.5 %copy-start.1 = (bf16[8,2,1024,128]{3,2,1,0:T(8,128)(2,1)S(1)}, bf16[8,2,1024,128]{3,2,1,0:T(8,128)(2,1)}, u32[]{:S(2)}) copy-start(bf16[8,2,1024,128]{3,2,1,0:T(8,128)(2,1)} %param.11) | copy-start | bytes 12582916
  104.9 5.3 %copy-start.4 = (bf16[8,2,1024,128]{3,2,1,0:T(8,128)(2,1)S(1)}, bf16[8,2,1024,128]{3,2,1,0:T(8,128)(2,1)}, u32[]{:S(2)}) copy-start(bf16[8,2,1024,128]{3,2,1,0:T(8,128)(2,1)} %param.12) | copy-start | bytes 12582916
Sparse Core Ops, SparseCore 0:
  8.9 19.4 all-gather.4
  29.9 58.2 all-gather.2
where the time goes:
time: 119 us; the launch traced here: 118 us
  waiting for transfers between devices  55 us (46%)
  blocking collectives  26.9 us (23%)
  local copies, waits for them, and re-layouts  14.7 us (12%)
  between operations  13.6 us (11%)
  matrix products  7.57 us (6%)
    all_gather x1, waiting for transfers between devices, on_device(): lax.all_gather(adapter_down_weight, 'replica', axis=0, tiled=True)  53.6 us
    all_gather x1, blocking collectives, on_device(): lax.all_gather(hidden_state_rows, 'tensor', axis=1, tiled=True)  15.1 us
    psum x1, blocking collectives, on_device(): reduced_rank_state = lax.psum(partial_low, 'tensor')  11.8 us
    unnamed x14, local copies, waits for them, and re-layouts  8.87 us
    dot_general x1, matrix products, on_device(): jnp.dot(lax.all_gather(hidden_state_rows, 'tensor', axis=1, tiled=True),...  4.71 us
    gather x1, local copies, waits for them, and re-layouts, on_device(): picked_in = jnp.take(every_in, row_adapter_index, axis=0)  3.99 us
  transfers between devices with their start and end apart: 2, of which 1 were waited for; matrix products, arithmetic and copies ran while one was open for 10% of the time, Pallas kernels for 0%

commit v1 on v0

--- a/solution.py
+++ b/solution.py
@@ -1,11 +1,15 @@
+import functools
 import math
 
 import jax
 import jax.numpy as jnp
 from jax import lax
+from jax.experimental import pallas as pl
+from jax.experimental.pallas import tpu as pltpu
 from jax.sharding import PartitionSpec as P
 
 adapter_scale = 2.0
+LANES = 128
 
 
 def rotate_keys(vectors, positions):
@@ -24,7 +28,264 @@
     )
 
 
+def dot(a, b):
+    return jnp.dot(a, b, preferred_element_type=jnp.float32)
+
+
+def project_kernel(
+    tensor_size, replica_size, pieces,
+    h_ref, ids_ref, weight_hbm, down_hbm, up_hbm, out_ref,
+    hs_own, hs_t, hs_r, ids_r, weight, down, up, expanded, total,
+    low_own, low_rx, delta_tx, delta_rx,
+    load_sem, send_sem, recv_sem,
+):
+    rows, local = h_ref.shape
+    blocks = local // LANES
+    half_blocks = blocks // 2
+    band = rows * pieces
+    wide = LANES * pieces
+    half_depth = half_blocks * wide
+    shard_depth = 2 * half_depth
+    rank2 = 32
+    adapters = down.shape[0] // rank2
+    per_tile = LANES // rank2
+    tiles = adapters // per_tile
+
+    me_t = lax.axis_index("tensor")
+    me_r = lax.axis_index("replica")
+
+    def t_at(step):
+        return lax.rem(me_t + step + tensor_size, tensor_size)
+
+    def r_at(step):
+        return lax.rem(me_r + step + replica_size, replica_size)
+
+    loads = [
+        pltpu.make_async_copy(down_hbm, down, load_sem.at[0]),
+        pltpu.make_async_copy(up_hbm, up, load_sem.at[1]),
+    ]
+    for d in range(tensor_size):
+        source = pl.ds(pl.multiple_of(t_at(-d) * shard_depth, shard_depth), shard_depth)
+        loads.append(
+            pltpu.make_async_copy(weight_hbm.at[source], weight.at[d], load_sem.at[2 + d])
+        )
+    for load in loads:
+        load.start()
+
+    barrier = pltpu.get_barrier_semaphore()
+    for d in range(1, tensor_size):
+        pl.semaphore_signal(barrier, inc=1, device_id={"tensor": t_at(d)},
+                            device_id_type=pl.DeviceIdType.MESH)
+    for d in range(1, replica_size):
+        pl.semaphore_signal(barrier, inc=1, device_id={"replica": r_at(d)},
+                            device_id_type=pl.DeviceIdType.MESH)
+
+    h32 = h_ref[...].astype(jnp.float32)
+    hs_own[...] = jnp.concatenate(
+        [h32[:, b * LANES:(b + 1) * LANES] for b in range(blocks)], axis=0
+    ).astype(jnp.bfloat16)
+    pl.semaphore_wait(barrier, tensor_size + replica_size - 2)
+
+    count = [0]
+
+    def remote(source, target, device):
+        slot = count[0]
+        count[0] += 1
+        copy = pltpu.make_async_remote_copy(
+            src_ref=source, dst_ref=target, send_sem=send_sem.at[slot],
+            recv_sem=recv_sem.at[slot], device_id=device,
+            device_id_type=pl.DeviceIdType.MESH,
+        )
+        copy.start()
+        return copy
+
+    ids_copies = [
+        remote(ids_ref, ids_r.at[d - 1], {"replica": r_at(d)}) for d in range(1, replica_size)
+    ]
+    r_copies = [
+        remote(hs_own, hs_r.at[d - 1], {"replica": r_at(d)}) for d in range(1, replica_size)
+    ]
+    t_copies = [
+        remote(hs_own, hs_t.at[d - 1], {"tensor": t_at(d)}) for d in range(1, tensor_size)
+    ]
+
+    lane_of = lax.broadcasted_iota(jnp.int32, (rows, wide), 1)
+    piece_shift = pieces.bit_length() - 1
+    row_of = lax.broadcasted_iota(jnp.int32, (LANES, wide), 0)
+    column_of = lax.broadcasted_iota(jnp.int32, (LANES, wide), 1)
+    spread = jnp.where(
+        lax.shift_right_logical(column_of, piece_shift) == row_of, 1.0, 0.0
+    ).astype(jnp.bfloat16)
+    piece_of = lane_of & (pieces - 1)
+
+    def expand(source, d):
+        repeated = dot(source, spread)
+        for b in range(blocks):
+            one = repeated[b * rows:(b + 1) * rows]
+            parts = [jnp.where(piece_of == j, one, 0.0) for j in range(pieces)]
+            half, at = divmod(b, half_blocks)
+            expanded[d, half * band:(half + 1) * band, at * wide:(at + 1) * wide] = (
+                jnp.concatenate(parts, axis=0).astype(jnp.bfloat16)
+            )
+
+    chunk = min(1024, half_depth)
+
+    def accumulate(d):
+        loads[2 + d].wait()
+
+        def body(i, acc):
+            at = pl.multiple_of(i * chunk, chunk)
+            right = jnp.concatenate(
+                [weight[d, pl.ds(at, chunk), :], weight[d, pl.ds(half_depth + at, chunk), :]],
+                axis=1,
+            )
+            return acc + dot(expanded[d, :, pl.ds(at, chunk)], right)
+
+        total[...] = lax.fori_loop(0, half_depth // chunk, body, total[...])
+
+    total[...] = jnp.zeros_like(total)
+    expand(hs_own[...], 0)
+
+    loads[0].wait()
+    for copy in ids_copies + r_copies:
+        copy.wait_recv()
+    stacks = [hs_own[...].astype(jnp.float32)] + [
+        hs_r[d - 1].astype(jnp.float32) for d in range(1, replica_size)
+    ]
+    all_rows = jnp.concatenate(
+        [
+            jnp.concatenate([s[b * rows:(b + 1) * rows] for s in stacks], axis=0).astype(
+                jnp.bfloat16
+            )
+            for b in range(blocks)
+        ],
+        axis=1,
+    )
+    low_all = lax.dot_general(
+        all_rows, down[...], (((1,), (1,)), ((), ())), preferred_element_type=jnp.float32
+    )
+    ids = jnp.concatenate(
+        [ids_ref[...]] + [ids_r[d - 1] for d in range(1, replica_size)], axis=0
+    ) - me_r * adapters
+    lane = lax.broadcasted_iota(jnp.int32, ids.shape, 1)
+    adapter_of = lax.shift_right_logical(lane, rank2.bit_length() - 1)
+    chosen = [ids == adapter_of + k * per_tile for k in range(tiles)]
+    low = jnp.zeros(ids.shape, jnp.float32)
+    for k in range(tiles):
+        low = low + jnp.where(chosen[k], low_all[:, k * LANES:(k + 1) * LANES], 0.0)
+    low_own[...] = low
+    low_copies = [
+        remote(low_own, low_rx.at[d - 1], {"tensor": t_at(d)}) for d in range(1, tensor_size)
+    ]
+
+    accumulate(0)
+
+    loads[1].wait()
+    for copy in low_copies:
+        copy.wait_recv()
+    for d in range(1, tensor_size):
+        low = low + low_rx[d - 1]
+    spread_low = jnp.concatenate([jnp.where(chosen[k], low, 0.0) for k in range(tiles)], axis=1)
+    which = lax.broadcasted_iota(jnp.int32, spread_low.shape, 1) & (rank2 - 1)
+    first = which < rank2 // 2
+    left = jnp.concatenate(
+        [jnp.where(first, spread_low, 0.0), jnp.where(first, 0.0, spread_low)], axis=0
+    )
+    top = left.astype(jnp.bfloat16)
+    rest = left - top.astype(jnp.float32)
+    middle = rest.astype(jnp.bfloat16)
+    bottom = (rest - middle.astype(jnp.float32)).astype(jnp.bfloat16)
+    delta = dot(top, up[...]) + (dot(middle, up[...]) + dot(bottom, up[...]))
+    group_rows = rows * replica_size
+    for d in range(replica_size):
+        delta_tx[d] = jnp.concatenate(
+            [
+                delta[
+                    (j % 2) * group_rows + d * rows:(j % 2) * group_rows + (d + 1) * rows,
+                    (j // 2) * LANES:(j // 2 + 1) * LANES,
+                ]
+                for j in range(pieces)
+            ],
+            axis=0,
+        )
+    delta_copies = [
+        remote(delta_tx.at[d], delta_rx.at[d - 1], {"replica": r_at(-d)})
+        for d in range(1, replica_size)
+    ]
+
+    for d in range(1, tensor_size):
+        t_copies[d - 1].wait_recv()
+        expand(hs_t[d - 1], d)
+        accumulate(d)
+
+    result = total[0:band, 0:LANES] + total[band:2 * band, LANES:2 * LANES]
+    update = delta_tx[0]
+    for d in range(1, replica_size):
+        delta_copies[d - 1].wait_recv()
+        update = update + delta_rx[d - 1]
+    out_ref[...] = result + adapter_scale * update
+    for copy in ids_copies + r_copies + t_copies + low_copies + delta_copies:
+        copy.wait_send()
+
+
+def project(tensor_size, replica_size, hidden, ids, weight, down, up):
+    rows, local = hidden.shape
+    width = weight.shape[0]
+    pieces = weight.shape[1] * weight.shape[2] // LANES
+    blocks = local // LANES
+    band = rows * pieces
+    weight = (
+        weight.reshape(width, 2, pieces // 2, LANES)
+        .transpose(0, 2, 1, 3)
+        .reshape(width * pieces, LANES)
+    )
+    adapters, _, rank2 = down.shape
+    down = down.transpose(0, 2, 1).reshape(adapters * rank2, local)
+    up = up.reshape(adapters * rank2, up.shape[3])
+    ids = jnp.broadcast_to(ids[:, None], (rows, LANES))
+    t1, r1 = tensor_size - 1, replica_size - 1
+    copies = 2 * t1 + 3 * r1
+    vmem = pl.BlockSpec(memory_space=pltpu.VMEM)
+    hbm = pl.BlockSpec(memory_space=pl.ANY)
+    stack = (blocks * rows, LANES)
+    group_rows = rows * replica_size
+    return pl.pallas_call(
+        functools.partial(project_kernel, tensor_size, replica_size, pieces),
+        out_shape=jax.ShapeDtypeStruct((band, LANES), jnp.float32),
+        in_specs=[vmem, vmem, hbm, hbm, hbm],
+        out_specs=vmem,
+        scratch_shapes=[
+            pltpu.VMEM(stack, jnp.bfloat16),
+            pltpu.VMEM((t1,) + stack, jnp.bfloat16),
+            pltpu.VMEM((r1,) + stack, jnp.bfloat16),
+            pltpu.VMEM((r1, rows, LANES), jnp.int32),
+            pltpu.VMEM((tensor_size, local * pieces, LANES), jnp.bfloat16),
+            pltpu.VMEM(down.shape, jnp.bfloat16),
+            pltpu.VMEM(up.shape, jnp.bfloat16),
+            pltpu.VMEM((tensor_size, 2 * band, local * pieces // 2), jnp.bfloat16),
+            pltpu.VMEM((2 * band, 2 * LANES), jnp.float32),
+            pltpu.VMEM((group_rows, LANES), jnp.float32),
+            pltpu.VMEM((t1, group_rows, LANES), jnp.float32),
+            pltpu.VMEM((replica_size, band, LANES), jnp.float32),
+            pltpu.VMEM((r1, band, LANES), jnp.float32),
+            pltpu.SemaphoreType.DMA((2 + tensor_size,)),
+            pltpu.SemaphoreType.DMA((copies,)),
+            pltpu.SemaphoreType.DMA((copies,)),
+        ],
+        compiler_params=pltpu.CompilerParams(
+            collective_id=0, has_side_effects=True, vmem_limit_bytes=30 << 20
+        ),
+        cost_estimate=pl.CostEstimate(
+            flops=2 * rows * width * pieces * LANES,
+            bytes_accessed=2 * (weight.size + down.size + up.size),
+            transcendentals=0,
+        ),
+    )(hidden, ids, weight, down, up)
+
+
 def on_device(
+    tensor_size,
+    replica_size,
     hidden_state_rows,
     queries,
     rotated_key_cache,
@@ -38,33 +299,18 @@
     request_row_count = hidden_state_rows.shape[0]
     shard_heads = rotated_key_cache.shape[1]
     head_width = rotated_key_cache.shape[3]
-    kv_width = shard_heads * head_width
-    weight_flat = key_value_weight.reshape(key_value_weight.shape[0], 2 * kv_width)
-    rank_width = adapter_down_weight.shape[2] // 2
-    base_projection = jnp.dot(
-        lax.all_gather(hidden_state_rows, "tensor", axis=1, tiled=True),
-        weight_flat,
-        preferred_element_type=jnp.float32,
-    )
-    every_in, every_out = (
-        lax.all_gather(adapter_down_weight, "replica", axis=0, tiled=True),
-        lax.all_gather(adapter_up_weight, "replica", axis=0, tiled=True),
-    )
-    picked_in = jnp.take(every_in, row_adapter_index, axis=0)
-    partial_low = jnp.einsum(
-        "rd,rdk->rk", hidden_state_rows, picked_in, preferred_element_type=jnp.float32
-    )
-    reduced_rank_state = lax.psum(partial_low, "tensor")
-    picked_out = jnp.take(every_out, row_adapter_index, axis=0).astype(jnp.float32)
-    adapter_update = jnp.einsum(
-        "rpj,rpjk->rpk",
-        reduced_rank_state.reshape(request_row_count, 2, rank_width),
-        picked_out,
-        precision=lax.Precision.HIGHEST,
-    ).reshape(request_row_count, 2 * kv_width)
-    projected_rows = (base_projection + adapter_scale * adapter_update).reshape(
-        request_row_count, 2, shard_heads, head_width
-    )
+    projected = project(
+        tensor_size,
+        replica_size,
+        hidden_state_rows,
+        row_adapter_index,
+        key_value_weight,
+        adapter_down_weight,
+        adapter_up_weight,
+    )
+    projected_rows = projected.reshape(
+        shard_heads, 2, request_row_count, head_width
+    ).transpose(2, 1, 0, 3)
     new_key = rotate_keys(projected_rows[:, 0], lengths).astype(jnp.bfloat16)
     new_value = projected_rows[:, 1].astype(jnp.bfloat16)
     group_size = queries.shape[1] // shard_heads
@@ -114,6 +360,7 @@
         P(("group", "replica"), None, None, "tensor"),
     )
     out_specs = P(("group", "replica"), "tensor")
+    body = functools.partial(on_device, mesh.shape["tensor"], mesh.shape["replica"])
     return jax.shard_map(
-        on_device, mesh=mesh, in_specs=in_specs, out_specs=out_specs, check_vma=False
-    )
+        body, mesh=mesh, in_specs=in_specs, out_specs=out_specs, check_vma=False
+    )

time: 119 us -> 29.6 us (0.25)
  waiting for transfers between devices: 55 us -> 0 us
  blocking collectives: 26.9 us -> 0 us
  Pallas kernels: 0 us -> 16.7 us
  between operations: 13.6 us -> 0.07 us
  local copies, waits for them, and re-layouts: 14.7 us -> 8.34 us
  matrix products: 7.57 us -> 2.14 us
  other arithmetic: 0.66 us -> 1.95 us
    all_gather x2 -> x0, waiting for transfers between devices: 53.6 us -> none  [the longest x1 53.6 us: on_device(): lax.all_gather(adapter_down_weight, 'replica', axis=0, tiled=True)]
    pallas_call x0 -> x1, Pallas kernels: none -> 16.7 us  [project(): pl.pallas_call(functools.partial(project_kernel, tensor_size, replica_siz...]
    all_gather x1 -> x0, blocking collectives: 15.1 us -> none  [on_device(): lax.all_gather(hidden_state_rows, 'tensor', axis=1, tiled=True)]
    psum x1 -> x0, blocking collectives: 11.8 us -> none  [on_device(): reduced_rank_state = lax.psum(partial_low, 'tensor')]
    gather x2 -> x0, local copies, waits for them, and re-layouts: 5.77 us -> none  [the longest x1 3.99 us: on_device(): picked_in = jnp.take(every_in, row_adapter_index, axis=0)]
    dot_general x3 -> x0, matrix products: 5.42 us -> none  [the longest x1 4.71 us: on_device(): jnp.dot(lax.all_gather(hidden_state_rows, 'tensor', axis=1, tiled=True),...]
    unnamed x2 -> x0, waiting for transfers between devices: 1.41 us -> none
    unnamed x14 -> x15, local copies, waits for them, and re-layouts: 8.87 us -> 7.6 us
  transfers between devices with their start and end apart: 2 -> 0, of which waited for: 1 -> 0; matrix products, arithmetic and copies ran while one was open for 10% -> 0% of each run, Pallas kernels for 0% -> 0%
where the time goes in v1:
time: 29.6 us; the launch traced here: 29.2 us
  Pallas kernels  16.7 us (56%)
  local copies, waits for them, and re-layouts  8.34 us (28%)
  matrix products  2.14 us (7%)
  other arithmetic  1.95 us (7%)
    pallas_call x1, Pallas kernels, project(): pl.pallas_call(functools.partial(project_kernel, tensor_size, replica_siz...  16.7 us
    unnamed x15, local copies, waits for them, and re-layouts  7.6 us
    dot_general x1, matrix products, on_device(): jnp.einsum('rkgd,rktd->rkgt', grouped, rotated_key_cache, preferred_eleme...  1.29 us
    lt x1, other arithmetic, on_device(): jnp.arange(cache_length, dtype=jnp.int32)[None, :] < lengths[:, None]  0.73 us
    broadcast_in_dim x1, local copies, waits for them, and re-layouts, project(): ids = jnp.broadcast_to(ids[:, None], (rows, LANES))  0.73 us
    dot_general x1, matrix products, on_device(): jnp.einsum('rkgt,rktd->rkgd', weights, cached_value_rows, preferred_eleme...  0.72 us
    convert_element_type x1, other arithmetic, rotate_keys(): angles = positions.astype(jnp.float32)[:, None] * frequency[None, :]  0.66 us

profile of v1, /device:TPU:0, one launch (start us, length us, event | category | flops | bytes accessed | tf_op | source)
XLA Modules:
  0.0 29.2 jit_solution(8311606917756589391)
XLA Ops:
  0.0 0.0 copy-start
  0.0 0.7 %convert_element_type.35 = f32[8]{0:T(128)S(1)} convert(s32[8]{0:T(128)} %param.13) | non-fusion elementwise | flops 8 | bytes 64 | tf_op jit(solution)/shard_map/convert_element_type | solution.py:21
  0.7 0.7 %broadcast_in_dim.12.ids_ref = s32[8,128]{1,0:T(8,128)S(1)} broadcast(s32[8]{0:T(128)} %param.14), dimensions={0} | broadcast | bytes 4128 | tf_op jit(solution)/shard_map/broadcast_in_dim | solution.py:245
  1.4 0.1 multiply_cosine_fusion
  1.5 0.7 %iota_compare_fusion = pred[8,1024]{1,0:T(8,128)(4,1)S(1)} fusion(s32[8]{0:T(128)} %param.13), kind=kLoop, calls=%fused_computation.14 | loop fusion | flops 8192 | bytes 8224 | tf_op jit(solution)/shard_map/lt | solution.py:326
  2.2 0.0 copy-start.1
  2.3 3.4 %copy-done.1 = bf16[8192,2,256]{2,1,0:T(2,128)(2,1)S(1)} copy-done((bf16[8192,2,256]{2,1,0:T(2,128)(2,1)S(1)}, bf16[8192,2,256]{2,1,0:T(2,128)(2,1)}, u32[]{:S(2)}) %copy-start.1) | copy-done | bytes 8388632
  5.6 0.0 copy-start.2
  5.6 1.6 %copy-done.2 = bf16[16,2048,32]{1,2,0:T(8,128)(2,1)S(1)} copy-done((bf16[16,2048,32]{1,2,0:T(8,128)(2,1)S(1)}, bf16[16,2048,32]{1,2,0:T(8,128)(2,1)}, u32[]{:S(2)}) %copy-start.2) | copy-done | bytes 2097176
  7.2 0.0 copy-start.3
  7.2 0.9 %copy-done.3 = bf16[16,2,16,256]{3,2,1,0:T(8,128)(2,1)S(1)} copy-done((bf16[16,2,16,256]{3,2,1,0:T(8,128)(2,1)S(1)}, bf16[16,2,16,256]{3,2,1,0:T(8,128)(2,1)}, u32[]{:S(2)}) %copy-start.3) | copy-done | bytes 262168
  8.2 0.0 copy-start.4
  8.2 0.8 %copy-done.4 = bf16[8,2048]{1,0:T(8,128)(2,1)S(1)} copy-done((bf16[8,2048]{1,0:T(8,128)(2,1)S(1)}, bf16[8,2048]{1,0:T(8,128)(2,1)}, u32[]{:S(2)}) %copy-start.4) | copy-done | bytes 32792
  8.9 0.0 copy-start.5
  8.9 16.7 %shard_map.91 = f32[32,128]{1,0:T(8,128)S(1)} custom-call(bf16[8,2048]{1,0:T(8,128)(2,1)S(1)} %copy-done.4, s32[8,128]{1,0:T(8,128)S(1)} %broadcast_in_dim.12.ids_ref, bf16[32768,128]{1,0:T(8,128)(2,1)S(1)} %bitcast.38, bf16[512,2048]{1,0:T(8,128)(2,1)S(1)} %bitcast.39, bf16[512,256]{1,0:T(8,128)(2,1)S(1)} %bitcast.40), custom_call_target="tpu_custom_call" | custom-call | flops 67108864 | bytes 10747904 | tf_op jit(solution)/shard_map/pallas_call | solution.py:252
  25.7 0.0 copy-start.6
  25.7 0.1 subtract_convert_fusion
  25.8 0.1 maximum_bitcast_fusion
  25.9 0.0 copy-done
  25.9 0.1 fusion.6
  26.0 0.0 copy-done.5
  26.0 1.3 %fusion.14 = (f32[8,2,8]{2,1,0:T(2,128)S(1)}, f32[8,2,8,1024]{3,2,1,0:T(8,128)S(1)}) fusion(bf16[8,2,1024,128]{3,2,1,0:T(8,128)(2,1)S(1)} %copy-done.5, bf16[8,16,128]{2,1,0:T(8,128)(2,1)S(1)} %copy-done, pred[8,1024]{1,0:T(8,128)(4,1)S(1)} %iota_compare_fusion), kind=kOutput, calls=%fused_computation.31 | convolution fusion | flops 33947520 | bytes 4760064 | tf_op jit(solution)/shard_map/rkgd,rktd->rkgt/dot_general | solution.py:321
  27.3 0.2 fusion.3
  27.6 0.3 copy-done.6
  27.9 0.7 %fusion.2 = bf16[1,8,16,128]{3,2,1,0:T(8,128)(2,1)S(1)} fusion(bf16[8,2,1024,128]{3,2,1,0:T(8,128)(2,1)S(1)} %copy-done.6, f32[8,2,8,1024]{3,2,1,0:T(8,128)S(1)} %get-tuple-element.12, f32[8,2,8]{2,1,0:T(2,128)S(1)} %get-tuple-element.6, f32[8,2,8]{2,1,0:T(2,128)S(1)} %multiply_maximum_fusion, f32[8,2,128]{2,1,0:T(2,128)S(1)} %copy.11, ...), kind=kOutput, calls=%fused_computation.4 | convolution fusion | flops 33996800 | bytes 4761088 | tf_op jit(solution)/shard_map/rkgt,rktd->rkgd/dot_general | solution.py:338
  28.6 0.6 %copy.18 = bf16[1,8,16,128]{3,1,2,0:T(8,128)(2,1)} copy(bf16[1,8,16,128]{3,2,1,0:T(8,128)(2,1)S(1)} %fusion.2) | data formatting | bytes 65536
  (6 shorter events, 0.1 us)
Async XLA Ops:
  0.0 25.9 %copy-start = (bf16[8,16,128]{2,1,0:T(8,128)(2,1)S(1)}, bf16[8,16,128]{2,1,0:T(8,128)(2,1)}, u32[]{:S(2)}) copy-start(bf16[8,16,128]{2,1,0:T(8,128)(2,1)} %param.10) | copy-start | bytes 98308
  2.2 3.4 %copy-start.1 = (bf16[8192,2,256]{2,1,0:T(2,128)(2,1)S(1)}, bf16[8192,2,256]{2,1,0:T(2,128)(2,1)}, u32[]{:S(2)}) copy-start(bf16[8192,2,256]{2,1,0:T(2,128)(2,1)} %param.15) | copy-start | bytes 25165828
  5.6 1.6 %copy-start.2 = (bf16[16,2048,32]{1,2,0:T(8,128)(2,1)S(1)}, bf16[16,2048,32]{1,2,0:T(8,128)(2,1)}, u32[]{:S(2)}) copy-start(bf16[16,2048,32]{1,2,0:T(8,128)(2,1)} %param.16) | copy-start | bytes 6291460
  7.2 0.9 %copy-start.3 = (bf16[16,2,16,256]{3,2,1,0:T(8,128)(2,1)S(1)}, bf16[16,2,16,256]{3,2,1,0:T(8,128)(2,1)}, u32[]{:S(2)}) copy-start(bf16[16,2,16,256]{3,2,1,0:T(8,128)(2,1)} %param.17) | copy-start | bytes 786436
  8.2 0.8 %copy-start.4 = (bf16[8,2048]{1,0:T(8,128)(2,1)S(1)}, bf16[8,2048]{1,0:T(8,128)(2,1)}, u32[]{:S(2)}) copy-start(bf16[8,2048]{1,0:T(8,128)(2,1)} %h_ref.1) | copy-start | bytes 98308
  8.9 17.1 %copy-start.5 = (bf16[8,2,1024,128]{3,2,1,0:T(8,128)(2,1)S(1)}, bf16[8,2,1024,128]{3,2,1,0:T(8,128)(2,1)}, u32[]{:S(2)}) copy-start(bf16[8,2,1024,128]{3,2,1,0:T(8,128)(2,1)} %param.11) | copy-start | bytes 12582916
  25.7 2.2 %copy-start.6 = (bf16[8,2,1024,128]{3,2,1,0:T(8,128)(2,1)S(1)}, bf16[8,2,1024,128]{3,2,1,0:T(8,128)(2,1)}, u32[]{:S(2)}) copy-start(bf16[8,2,1024,128]{3,2,1,0:T(8,128)(2,1)} %param.12) | copy-start | bytes 12582916

commit v2 on v1

--- a/solution.py
+++ b/solution.py
@@ -12,20 +12,11 @@
 LANES = 128
 
 
-def rotate_keys(vectors, positions):
-    head_width = vectors.shape[-1]
-    half_size = head_width // 2
-    frequency = jnp.exp(
-        jnp.arange(half_size, dtype=jnp.float32) * (-2.0 * math.log(500000.0) / head_width)
-    )
-    angles = positions.astype(jnp.float32)[:, None] * frequency[None, :]
-    cosine = jnp.cos(angles)[:, None, :]
-    sine = jnp.sin(angles)[:, None, :]
-    front_part = vectors[..., :half_size]
-    back_part = vectors[..., half_size:]
-    return jnp.concatenate(
-        [front_part * cosine - back_part * sine, back_part * cosine + front_part * sine], axis=-1
-    )
+def rotate_keys(vectors, cosine, sine):
+    half_size = vectors.shape[1] // 2
+    lane = lax.broadcasted_iota(jnp.int32, vectors.shape, 1)
+    swapped = pltpu.roll(vectors, half_size, 1)
+    return vectors * cosine + jnp.where(lane < half_size, -swapped, swapped) * sine
 
 
 def dot(a, b):
@@ -34,8 +25,8 @@
 
 def project_kernel(
     tensor_size, replica_size, pieces,
-    h_ref, ids_ref, weight_hbm, down_hbm, up_hbm, out_ref,
-    hs_own, hs_t, hs_r, ids_r, weight, down, up, expanded, total,
+    h_ref, query_ref, lengths_ref, index_ref, key_hbm, value_hbm, weight_hbm, down_hbm, up_hbm,
+    out_ref, ids_ref, keys, values, query32, mixed, peak, mass, hs_own, hs_t, hs_r, ids_r, weight, down, up, expanded, total,
     low_own, low_rx, delta_tx, delta_rx,
     load_sem, send_sem, recv_sem,
 ):
@@ -69,7 +60,19 @@
         loads.append(
             pltpu.make_async_copy(weight_hbm.at[source], weight.at[d], load_sem.at[2 + d])
         )
-    for load in loads:
+    heads = keys.shape[1]
+    row_half = rows // 2
+    cache_loads = []
+    for part in range(2):
+        span = pl.ds(part * row_half, row_half)
+        for source, target in ((key_hbm, keys), (value_hbm, values)):
+            cache_loads.append(
+                pltpu.make_async_copy(
+                    source.at[span], target.at[span],
+                    load_sem.at[2 + tensor_size + len(cache_loads)],
+                )
+            )
+    for load in loads[:2] + cache_loads + loads[2:]:
         load.start()
 
     barrier = pltpu.get_barrier_semaphore()
@@ -84,6 +87,8 @@
     hs_own[...] = jnp.concatenate(
         [h32[:, b * LANES:(b + 1) * LANES] for b in range(blocks)], axis=0
     ).astype(jnp.bfloat16)
+    for r in range(rows):
+        ids_ref[r:r + 1, :] = jnp.full((1, LANES), index_ref[r], jnp.int32)
     pl.semaphore_wait(barrier, tensor_size + replica_size - 2)
 
     count = [0]
@@ -143,8 +148,54 @@
 
         total[...] = lax.fori_loop(0, half_depth // chunk, body, total[...])
 
+    group_size = query_ref.shape[1] // heads
+    head_width = query_ref.shape[2]
+    cache = keys.shape[2]
+    scale = head_width ** (-0.5)
+
+    def attend(r):
+        query = query_ref[r].astype(jnp.float32)
+        query32[r] = query
+        if heads > 1:
+            owner = lax.broadcasted_iota(jnp.int32, query.shape, 0)
+            query = jnp.concatenate(
+                [
+                    jnp.where(
+                        (owner >= c * group_size) & (owner < (c + 1) * group_size), query, 0.0
+                    )
+                    for c in range(heads)
+                ],
+                axis=1,
+            )
+        key_row = jnp.concatenate([keys[r, c] for c in range(heads)], axis=1)
+        value_row = jnp.concatenate([values[r, c] for c in range(heads)], axis=1)
+        scores = lax.dot_general(
+            query.astype(jnp.bfloat16), key_row, (((1,), (1,)), ((), ())),
+            preferred_element_type=jnp.float32,
+        ) * scale
+        position = lax.broadcasted_iota(jnp.int32, scores.shape, 1)
+        scores = jnp.where(position < lengths_ref[r], scores, -1e30)
+        top = jnp.max(scores, axis=1, keepdims=True)
+        raw = jnp.exp(scores - top)
+        both = dot(raw.astype(jnp.bfloat16), value_row)
+        mixed[r] = jnp.concatenate(
+            [
+                both[c * group_size:(c + 1) * group_size, c * head_width:(c + 1) * head_width]
+                for c in range(heads)
+            ],
+            axis=0,
+        )
+        wide_shape = (heads * group_size, head_width)
+        peak[r] = jnp.broadcast_to(top, wide_shape)
+        mass[r] = jnp.broadcast_to(jnp.sum(raw, axis=1, keepdims=True), wide_shape)
+
     total[...] = jnp.zeros_like(total)
     expand(hs_own[...], 0)
+
+    for load in cache_loads[:2]:
+        load.wait()
+    for r in range(row_half):
+        attend(r)
 
     loads[0].wait()
     for copy in ids_copies + r_copies:
@@ -178,7 +229,10 @@
         remote(low_own, low_rx.at[d - 1], {"tensor": t_at(d)}) for d in range(1, tensor_size)
     ]
 
-    accumulate(0)
+    for load in cache_loads[2:]:
+        load.wait()
+    for r in range(row_half, rows):
+        attend(r)
 
     loads[1].wait()
     for copy in low_copies:
@@ -213,6 +267,7 @@
         for d in range(1, replica_size)
     ]
 
+    accumulate(0)
     for d in range(1, tensor_size):
         t_copies[d - 1].wait_recv()
         expand(hs_t[d - 1], d)
@@ -223,12 +278,36 @@
     for d in range(1, replica_size):
         delta_copies[d - 1].wait_recv()
         update = update + delta_rx[d - 1]
-    out_ref[...] = result + adapter_scale * update
+    projected = result + adapter_scale * update
+
+    position = jnp.concatenate(
+        [jnp.full((1, head_width), lengths_ref[r], jnp.int32) for r in range(rows)], axis=0
+    ).astype(jnp.float32)
+    lane = lax.broadcasted_iota(jnp.int32, (rows, head_width), 1) & (head_width // 2 - 1)
+    frequency = jnp.exp(lane.astype(jnp.float32) * (-2.0 * math.log(500000.0) / head_width))
+    cosine, sine = jnp.cos(position * frequency), jnp.sin(position * frequency)
+    outputs = []
+    for c in range(heads):
+        at = 2 * c * rows
+        new_key = rotate_keys(projected[at:at + rows], cosine, sine)
+        new_key = new_key.astype(jnp.bfloat16).astype(jnp.float32)
+        new_value = projected[at + rows:at + 2 * rows].astype(jnp.bfloat16).astype(jnp.float32)
+        for h in range(c * group_size, (c + 1) * group_size):
+            fresh = jnp.sum(query32[:, h, :] * new_key, axis=1, keepdims=True) * scale
+            old_peak = peak[:, h, :]
+            new_peak = jnp.maximum(old_peak, fresh)
+            keep = jnp.exp(old_peak - new_peak)
+            fresh_raw = jnp.exp(fresh - new_peak)
+            outputs.append(
+                (mixed[:, h, :] * keep + fresh_raw * new_value)
+                / (mass[:, h, :] * keep + fresh_raw)
+            )
+    out_ref[...] = jnp.concatenate(outputs, axis=1).astype(out_ref.dtype)
     for copy in ids_copies + r_copies + t_copies + low_copies + delta_copies:
         copy.wait_send()
 
 
-def project(tensor_size, replica_size, hidden, ids, weight, down, up):
+def project(tensor_size, replica_size, hidden, queries, keys, values, lengths, ids, weight, down, up):
     rows, local = hidden.shape
     width = weight.shape[0]
     pieces = weight.shape[1] * weight.shape[2] // LANES
@@ -242,19 +321,28 @@
     adapters, _, rank2 = down.shape
     down = down.transpose(0, 2, 1).reshape(adapters * rank2, local)
     up = up.reshape(adapters * rank2, up.shape[3])
-    ids = jnp.broadcast_to(ids[:, None], (rows, LANES))
     t1, r1 = tensor_size - 1, replica_size - 1
     copies = 2 * t1 + 3 * r1
     vmem = pl.BlockSpec(memory_space=pltpu.VMEM)
+    smem = pl.BlockSpec(memory_space=pltpu.SMEM)
     hbm = pl.BlockSpec(memory_space=pl.ANY)
     stack = (blocks * rows, LANES)
     group_rows = rows * replica_size
     return pl.pallas_call(
         functools.partial(project_kernel, tensor_size, replica_size, pieces),
-        out_shape=jax.ShapeDtypeStruct((band, LANES), jnp.float32),
-        in_specs=[vmem, vmem, hbm, hbm, hbm],
+        out_shape=jax.ShapeDtypeStruct(
+            (rows, queries.shape[1] * queries.shape[2]), jnp.bfloat16
+        ),
+        in_specs=[vmem, vmem, smem, smem, hbm, hbm, hbm, hbm, hbm],
         out_specs=vmem,
         scratch_shapes=[
+            pltpu.VMEM((rows, LANES), jnp.int32),
+            pltpu.VMEM(keys.shape, jnp.bfloat16),
+            pltpu.VMEM(values.shape, jnp.bfloat16),
+            pltpu.VMEM(queries.shape, jnp.float32),
+            pltpu.VMEM(queries.shape, jnp.float32),
+            pltpu.VMEM(queries.shape, jnp.float32),
+            pltpu.VMEM(queries.shape, jnp.float32),
             pltpu.VMEM(stack, jnp.bfloat16),
             pltpu.VMEM((t1,) + stack, jnp.bfloat16),
             pltpu.VMEM((r1,) + stack, jnp.bfloat16),
@@ -268,83 +356,19 @@
             pltpu.VMEM((t1, group_rows, LANES), jnp.float32),
             pltpu.VMEM((replica_size, band, LANES), jnp.float32),
             pltpu.VMEM((r1, band, LANES), jnp.float32),
-            pltpu.SemaphoreType.DMA((2 + tensor_size,)),
+            pltpu.SemaphoreType.DMA((6 + tensor_size,)),
             pltpu.SemaphoreType.DMA((copies,)),
             pltpu.SemaphoreType.DMA((copies,)),
         ],
         compiler_params=pltpu.CompilerParams(
-            collective_id=0, has_side_effects=True, vmem_limit_bytes=30 << 20
+            collective_id=0, has_side_effects=True, vmem_limit_bytes=58 << 20
         ),
         cost_estimate=pl.CostEstimate(
             flops=2 * rows * width * pieces * LANES,
             bytes_accessed=2 * (weight.size + down.size + up.size),
             transcendentals=0,
         ),
-    )(hidden, ids, weight, down, up)
-
-
-def on_device(
-    tensor_size,
-    replica_size,
-    hidden_state_rows,
-    queries,
-    rotated_key_cache,
-    cached_value_rows,
-    lengths,
-    row_adapter_index,
-    key_value_weight,
-    adapter_down_weight,
-    adapter_up_weight,
-):
-    request_row_count = hidden_state_rows.shape[0]
-    shard_heads = rotated_key_cache.shape[1]
-    head_width = rotated_key_cache.shape[3]
-    projected = project(
-        tensor_size,
-        replica_size,
-        hidden_state_rows,
-        row_adapter_index,
-        key_value_weight,
-        adapter_down_weight,
-        adapter_up_weight,
-    )
-    projected_rows = projected.reshape(
-        shard_heads, 2, request_row_count, head_width
-    ).transpose(2, 1, 0, 3)
-    new_key = rotate_keys(projected_rows[:, 0], lengths).astype(jnp.bfloat16)
-    new_value = projected_rows[:, 1].astype(jnp.bfloat16)
-    group_size = queries.shape[1] // shard_heads
-    score_scale = head_width ** (-0.5)
-    grouped = queries.reshape(request_row_count, shard_heads, group_size, head_width)
-    cache_length = rotated_key_cache.shape[2]
-    scores = (
-        jnp.einsum(
-            "rkgd,rktd->rkgt", grouped, rotated_key_cache, preferred_element_type=jnp.float32
-        )
-        * score_scale
-    )
-    visible = jnp.arange(cache_length, dtype=jnp.int32)[None, :] < lengths[:, None]
-    scores = jnp.where(visible[:, None, None, :], scores, -1e30)
-    fresh_score = (
-        jnp.einsum("rkgd,rkd->rkg", grouped, new_key, preferred_element_type=jnp.float32)
-        * score_scale
-    )
-    peak_score = jnp.maximum(jnp.max(scores, axis=-1), fresh_score)
-    weights_raw = jnp.exp(scores - peak_score[..., None])
-    fresh_raw = jnp.exp(fresh_score - peak_score)
-    denominator = jnp.sum(weights_raw, axis=-1) + fresh_raw
-    weights = (weights_raw / denominator[..., None]).astype(jnp.bfloat16)
-    fresh_weight = (fresh_raw / denominator).astype(jnp.bfloat16)
-    mixed = jnp.einsum(
-        "rkgt,rktd->rkgd", weights, cached_value_rows, preferred_element_type=jnp.float32
-    )
-    mixed = (
-        mixed
-        + fresh_weight.astype(jnp.float32)[..., None] * new_value.astype(jnp.float32)[:, :, None, :]
-    )
-    return mixed.reshape(request_row_count, shard_heads * group_size * head_width).astype(
-        jnp.bfloat16
-    )
+    )(hidden, queries, lengths, ids, keys, values, weight, down, up)
 
 
 def solution(mesh):
@@ -360,7 +384,7 @@
         P(("group", "replica"), None, None, "tensor"),
     )
     out_specs = P(("group", "replica"), "tensor")
-    body = functools.partial(on_device, mesh.shape["tensor"], mesh.shape["replica"])
+    body = functools.partial(project, mesh.shape["tensor"], mesh.shape["replica"])
     return jax.shard_map(
         body, mesh=mesh, in_specs=in_specs, out_specs=out_specs, check_vma=False
     )

time: 29.6 us -> 20.2 us (0.68)
  local copies, waits for them, and re-layouts: 8.34 us -> 1.38 us
  matrix products: 2.14 us -> 0 us
  other arithmetic: 1.95 us -> 0 us
  Pallas kernels: 16.7 us -> 18.5 us
    unnamed x15 -> x1, local copies, waits for them, and re-layouts: 7.6 us -> 1.38 us
    dot_general x3 -> x0, matrix products: 2.14 us -> none  [the longest x1 1.29 us: on_device(): jnp.einsum('rkgd,rktd->rkgt', grouped, rotated_key_cache, preferred_eleme...]
    pallas_call x1, Pallas kernels: 16.7 us -> 18.5 us  [project(): pl.pallas_call(functools.partial(project_kernel, tensor_size, replica_siz...]
    lt x1 -> x0, other arithmetic: 0.73 us -> none  [on_device(): jnp.arange(cache_length, dtype=jnp.int32)[None, :] < lengths[:, None]]
    broadcast_in_dim x1 -> x0, local copies, waits for them, and re-layouts: 0.73 us -> none  [project(): ids = jnp.broadcast_to(ids[:, None], (rows, LANES))]
    convert_element_type x3 -> x0, other arithmetic: 0.69 us -> none  [the longest x1 0.66 us: rotate_keys(): angles = positions.astype(jnp.float32)[:, None] * frequency[None, :]]
where the time goes in v2:
time: 20.2 us; the launch traced here: 19.9 us
  Pallas kernels  18.5 us (92%)
  local copies, waits for them, and re-layouts  1.38 us (7%)
    pallas_call x1, Pallas kernels, project(): pl.pallas_call(functools.partial(project_kernel, tensor_size, replica_siz...  18.5 us
    unnamed x1, local copies, waits for them, and re-layouts  1.38 us

profile of v2, /device:TPU:0, one launch (start us, length us, event | category | flops | bytes accessed | tf_op | source)
XLA Modules:
  0.0 19.9 jit_solution(5675439485446257882)
XLA Ops:
  0.0 18.5 %shard_map.91 = bf16[8,2048]{1,0:T(8,128)(2,1)} custom-call(bf16[8,2048]{1,0:T(8,128)(2,1)} %h_ref.1, bf16[8,16,128]{2,1,0:T(8,128)(2,1)} %query_ref.1, s32[8]{0:T(128)} %lengths_ref.1, s32[8]{0:T(128)} %index_ref.1, bf16[8,2,1024,128]{3,2,1,0:T(8,128)(2,1)} %key_hbm.1, bf16[8,2,1024,128]{3,2,1,0:T(8,128)(2,1)} %value_hbm.1, bf16[32768,128]{1,0:T(8,128)(2,1)} %bitcast.9, ...), custom_call_target="tpu_custom_call" | custom-call | flops 67108864 | bytes 10747904 | tf_op jit(solution)/shard_map/pallas_call | solution.py:331
  18.6 1.4 %copy.12 = bf16[8,2048]{1,0:T(8,128)(2,1)} copy(bf16[8,2048]{1,0:T(8,128)(2,1)} %shard_map.91) | data formatting | bytes 65536

commit v3 on v2

--- a/solution.py
+++ b/solution.py
@@ -72,7 +72,7 @@
                     load_sem.at[2 + tensor_size + len(cache_loads)],
                 )
             )
-    for load in loads[:2] + cache_loads + loads[2:]:
+    for load in loads[2:3] + loads[:2] + cache_loads + loads[3:]:
         load.start()
 
     barrier = pltpu.get_barrier_semaphore()
@@ -89,6 +89,34 @@
     ).astype(jnp.bfloat16)
     for r in range(rows):
         ids_ref[r:r + 1, :] = jnp.full((1, LANES), index_ref[r], jnp.int32)
+    lane_of = lax.broadcasted_iota(jnp.int32, (rows, wide), 1)
+    piece_shift = pieces.bit_length() - 1
+    row_of = lax.broadcasted_iota(jnp.int32, (LANES, wide), 0)
+    column_of = lax.broadcasted_iota(jnp.int32, (LANES, wide), 1)
+    spread = jnp.where(
+        lax.shift_right_logical(column_of, piece_shift) == row_of, 1.0, 0.0
+    ).astype(jnp.bfloat16)
+    piece_of = lane_of & (pieces - 1)
+
+    def expand(source, d):
+        repeated = dot(source, spread)
+        for b in range(blocks):
+            one = repeated[b * rows:(b + 1) * rows]
+            parts = [jnp.where(piece_of == j, one, 0.0) for j in range(pieces)]
+            half, at = divmod(b, half_blocks)
+            expanded[d, half * band:(half + 1) * band, at * wide:(at + 1) * wide] = (
+                jnp.concatenate(parts, axis=0).astype(jnp.bfloat16)
+            )
+
+    expand(hs_own[...], 0)
+    total[...] = jnp.zeros_like(total)
+    head_width = query_ref.shape[2]
+    position = jnp.concatenate(
+        [jnp.full((1, head_width), lengths_ref[r], jnp.int32) for r in range(rows)], axis=0
+    ).astype(jnp.float32)
+    lane = lax.broadcasted_iota(jnp.int32, (rows, head_width), 1) & (head_width // 2 - 1)
+    frequency = jnp.exp(lane.astype(jnp.float32) * (-2.0 * math.log(500000.0) / head_width))
+    cosine, sine = jnp.cos(position * frequency), jnp.sin(position * frequency)
     pl.semaphore_wait(barrier, tensor_size + replica_size - 2)
 
     count = [0]
@@ -114,25 +142,6 @@
         remote(hs_own, hs_t.at[d - 1], {"tensor": t_at(d)}) for d in range(1, tensor_size)
     ]
 
-    lane_of = lax.broadcasted_iota(jnp.int32, (rows, wide), 1)
-    piece_shift = pieces.bit_length() - 1
-    row_of = lax.broadcasted_iota(jnp.int32, (LANES, wide), 0)
-    column_of = lax.broadcasted_iota(jnp.int32, (LANES, wide), 1)
-    spread = jnp.where(
-        lax.shift_right_logical(column_of, piece_shift) == row_of, 1.0, 0.0
-    ).astype(jnp.bfloat16)
-    piece_of = lane_of & (pieces - 1)
-
-    def expand(source, d):
-        repeated = dot(source, spread)
-        for b in range(blocks):
-            one = repeated[b * rows:(b + 1) * rows]
-            parts = [jnp.where(piece_of == j, one, 0.0) for j in range(pieces)]
-            half, at = divmod(b, half_blocks)
-            expanded[d, half * band:(half + 1) * band, at * wide:(at + 1) * wide] = (
-                jnp.concatenate(parts, axis=0).astype(jnp.bfloat16)
-            )
-
     chunk = min(1024, half_depth)
 
     def accumulate(d):
@@ -149,7 +158,6 @@
         total[...] = lax.fori_loop(0, half_depth // chunk, body, total[...])
 
     group_size = query_ref.shape[1] // heads
-    head_width = query_ref.shape[2]
     cache = keys.shape[2]
     scale = head_width ** (-0.5)
 
@@ -189,13 +197,8 @@
         peak[r] = jnp.broadcast_to(top, wide_shape)
         mass[r] = jnp.broadcast_to(jnp.sum(raw, axis=1, keepdims=True), wide_shape)
 
-    total[...] = jnp.zeros_like(total)
-    expand(hs_own[...], 0)
-
-    for load in cache_loads[:2]:
-        load.wait()
-    for r in range(row_half):
-        attend(r)
+
+    accumulate(0)
 
     loads[0].wait()
     for copy in ids_copies + r_copies:
@@ -224,21 +227,46 @@
     low = jnp.zeros(ids.shape, jnp.float32)
     for k in range(tiles):
         low = low + jnp.where(chosen[k], low_all[:, k * LANES:(k + 1) * LANES], 0.0)
+    quarter = lax.shift_right_logical(
+        lax.broadcasted_iota(jnp.int32, (rows, LANES), 1), rank2.bit_length() - 1
+    )
+
+    def fill(x):
+        full = x
+        for turn in range(1, per_tile):
+            full = full + pltpu.roll(x, turn * rank2, 1)
+        return full
+
+    filled = fill(low)
+    packed = []
+    for base in range(0, replica_size, per_tile):
+        one = jnp.zeros((rows, LANES), jnp.float32)
+        for g in range(per_tile):
+            at = (base + g) * rows
+            one = jnp.where(quarter == g, filled[at:at + rows], one)
+        packed.append(one)
+    low = jnp.concatenate(packed, axis=0)
     low_own[...] = low
     low_copies = [
         remote(low_own, low_rx.at[d - 1], {"tensor": t_at(d)}) for d in range(1, tensor_size)
     ]
 
-    for load in cache_loads[2:]:
-        load.wait()
-    for r in range(row_half, rows):
-        attend(r)
+    for part in range(2):
+        for load in cache_loads[2 * part:2 * part + 2]:
+            load.wait()
+        for r in range(part * row_half, (part + 1) * row_half):
+            attend(r)
 
     loads[1].wait()
     for copy in low_copies:
         copy.wait_recv()
     for d in range(1, tensor_size):
         low = low + low_rx[d - 1]
+    unpacked = []
+    for d in range(replica_size):
+        at = (d // per_tile) * rows
+        unpacked.append(jnp.where(quarter == d % per_tile, low[at:at + rows], 0.0))
+    low = fill(jnp.concatenate(unpacked, axis=0))
     spread_low = jnp.concatenate([jnp.where(chosen[k], low, 0.0) for k in range(tiles)], axis=1)
     which = lax.broadcasted_iota(jnp.int32, spread_low.shape, 1) & (rank2 - 1)
     first = which < rank2 // 2
@@ -267,7 +295,6 @@
         for d in range(1, replica_size)
     ]
 
-    accumulate(0)
     for d in range(1, tensor_size):
         t_copies[d - 1].wait_recv()
         expand(hs_t[d - 1], d)
@@ -280,12 +307,6 @@
         update = update + delta_rx[d - 1]
     projected = result + adapter_scale * update
 
-    position = jnp.concatenate(
-        [jnp.full((1, head_width), lengths_ref[r], jnp.int32) for r in range(rows)], axis=0
-    ).astype(jnp.float32)
-    lane = lax.broadcasted_iota(jnp.int32, (rows, head_width), 1) & (head_width // 2 - 1)
-    frequency = jnp.exp(lane.astype(jnp.float32) * (-2.0 * math.log(500000.0) / head_width))
-    cosine, sine = jnp.cos(position * frequency), jnp.sin(position * frequency)
     outputs = []
     for c in range(heads):
         at = 2 * c * rows
@@ -327,11 +348,11 @@
     smem = pl.BlockSpec(memory_space=pltpu.SMEM)
     hbm = pl.BlockSpec(memory_space=pl.ANY)
     stack = (blocks * rows, LANES)
-    group_rows = rows * replica_size
+    group_rows = rows * replica_size * 32 // LANES
     return pl.pallas_call(
         functools.partial(project_kernel, tensor_size, replica_size, pieces),
         out_shape=jax.ShapeDtypeStruct(
-            (rows, queries.shape[1] * queries.shape[2]), jnp.bfloat16
+            (rows, queries.shape[1] * queries.shape[2]), jnp.float32
         ),
         in_specs=[vmem, vmem, smem, smem, hbm, hbm, hbm, hbm, hbm],
         out_specs=vmem,
@@ -368,7 +389,7 @@
             bytes_accessed=2 * (weight.size + down.size + up.size),
             transcendentals=0,
         ),
-    )(hidden, queries, lengths, ids, keys, values, weight, down, up)
+    )(hidden, queries, lengths, ids, keys, values, weight, down, up).astype(jnp.bfloat16)
 
 
 def solution(mesh):

time: 20.2 us -> 20.1 us (level)
  other arithmetic: 0 us -> 1.46 us
  local copies, waits for them, and re-layouts: 1.38 us -> 0 us
    convert_element_type x0 -> x1, other arithmetic: none -> 1.46 us  [project(): return pl.pallas_call(functools.partial(project_kernel, tensor_size, repl...]
    unnamed x1 -> x0, local copies, waits for them, and re-layouts: 1.38 us -> none
where the time goes in v3:
time: 20.1 us; the launch traced here: 19.9 us
  Pallas kernels  18.4 us (92%)
  other arithmetic  1.46 us (7%)
    pallas_call x1, Pallas kernels, project(): pl.pallas_call(functools.partial(project_kernel, tensor_size, replica_siz...  18.4 us
    convert_element_type x1, other arithmetic, project(): return pl.pallas_call(functools.partial(project_kernel, tensor_size, repl...  1.46 us

profile of v3, /device:TPU:0, one launch (start us, length us, event | category | flops | bytes accessed | tf_op | source)
XLA Modules:
  0.0 19.9 jit_solution(17879454629131713734)
XLA Ops:
  0.0 18.4 %shard_map.91 = f32[8,2048]{1,0:T(8,128)} custom-call(bf16[8,2048]{1,0:T(8,128)(2,1)} %h_ref.1, bf16[8,16,128]{2,1,0:T(8,128)(2,1)} %query_ref.1, s32[8]{0:T(128)} %lengths_ref.1, s32[8]{0:T(128)} %index_ref.1, bf16[8,2,1024,128]{3,2,1,0:T(8,128)(2,1)} %key_hbm.1, bf16[8,2,1024,128]{3,2,1,0:T(8,128)(2,1)} %value_hbm.1, bf16[32768,128]{1,0:T(8,128)(2,1)} %bitcast.9, ...), custom_call_target="tpu_custom_call" | custom-call | flops 67108864 | bytes 10747904 | tf_op jit(solution)/shard_map/pallas_call | solution.py:352
  18.4 1.5 %convert_element_type.3 = bf16[8,2048]{1,0:T(8,128)(2,1)} convert(f32[8,2048]{1,0:T(8,128)} %shard_map.91) | non-fusion elementwise | flops 16384 | bytes 98304 | tf_op jit(solution)/shard_map/convert_element_type | solution.py:392

commit v4 on v3

--- a/solution.py
+++ b/solution.py
@@ -51,6 +51,14 @@
     def r_at(step):
         return lax.rem(me_r + step + replica_size, replica_size)
 
+    barrier = pltpu.get_barrier_semaphore()
+    for d in range(1, tensor_size):
+        pl.semaphore_signal(barrier, inc=1, device_id={"tensor": t_at(d)},
+                            device_id_type=pl.DeviceIdType.MESH)
+    for d in range(1, replica_size):
+        pl.semaphore_signal(barrier, inc=1, device_id={"replica": r_at(d)},
+                            device_id_type=pl.DeviceIdType.MESH)
+
     loads = [
         pltpu.make_async_copy(down_hbm, down, load_sem.at[0]),
         pltpu.make_async_copy(up_hbm, up, load_sem.at[1]),
@@ -75,48 +83,12 @@
     for load in loads[2:3] + loads[:2] + cache_loads + loads[3:]:
         load.start()
 
-    barrier = pltpu.get_barrier_semaphore()
-    for d in range(1, tensor_size):
-        pl.semaphore_signal(barrier, inc=1, device_id={"tensor": t_at(d)},
-                            device_id_type=pl.DeviceIdType.MESH)
-    for d in range(1, replica_size):
-        pl.semaphore_signal(barrier, inc=1, device_id={"replica": r_at(d)},
-                            device_id_type=pl.DeviceIdType.MESH)
-
     h32 = h_ref[...].astype(jnp.float32)
     hs_own[...] = jnp.concatenate(
         [h32[:, b * LANES:(b + 1) * LANES] for b in range(blocks)], axis=0
     ).astype(jnp.bfloat16)
     for r in range(rows):
         ids_ref[r:r + 1, :] = jnp.full((1, LANES), index_ref[r], jnp.int32)
-    lane_of = lax.broadcasted_iota(jnp.int32, (rows, wide), 1)
-    piece_shift = pieces.bit_length() - 1
-    row_of = lax.broadcasted_iota(jnp.int32, (LANES, wide), 0)
-    column_of = lax.broadcasted_iota(jnp.int32, (LANES, wide), 1)
-    spread = jnp.where(
-        lax.shift_right_logical(column_of, piece_shift) == row_of, 1.0, 0.0
-    ).astype(jnp.bfloat16)
-    piece_of = lane_of & (pieces - 1)
-
-    def expand(source, d):
-        repeated = dot(source, spread)
-        for b in range(blocks):
-            one = repeated[b * rows:(b + 1) * rows]
-            parts = [jnp.where(piece_of == j, one, 0.0) for j in range(pieces)]
-            half, at = divmod(b, half_blocks)
-            expanded[d, half * band:(half + 1) * band, at * wide:(at + 1) * wide] = (
-                jnp.concatenate(parts, axis=0).astype(jnp.bfloat16)
-            )
-
-    expand(hs_own[...], 0)
-    total[...] = jnp.zeros_like(total)
-    head_width = query_ref.shape[2]
-    position = jnp.concatenate(
-        [jnp.full((1, head_width), lengths_ref[r], jnp.int32) for r in range(rows)], axis=0
-    ).astype(jnp.float32)
-    lane = lax.broadcasted_iota(jnp.int32, (rows, head_width), 1) & (head_width // 2 - 1)
-    frequency = jnp.exp(lane.astype(jnp.float32) * (-2.0 * math.log(500000.0) / head_width))
-    cosine, sine = jnp.cos(position * frequency), jnp.sin(position * frequency)
     pl.semaphore_wait(barrier, tensor_size + replica_size - 2)
 
     count = [0]
@@ -138,10 +110,35 @@
     r_copies = [
         remote(hs_own, hs_r.at[d - 1], {"replica": r_at(d)}) for d in range(1, replica_size)
     ]
-    t_copies = [
-        remote(hs_own, hs_t.at[d - 1], {"tensor": t_at(d)}) for d in range(1, tensor_size)
-    ]
-
+
+    lane_of = lax.broadcasted_iota(jnp.int32, (rows, wide), 1)
+    piece_shift = pieces.bit_length() - 1
+    row_of = lax.broadcasted_iota(jnp.int32, (LANES, wide), 0)
+    column_of = lax.broadcasted_iota(jnp.int32, (LANES, wide), 1)
+    spread = jnp.where(
+        lax.shift_right_logical(column_of, piece_shift) == row_of, 1.0, 0.0
+    ).astype(jnp.bfloat16)
+    piece_of = lane_of & (pieces - 1)
+
+    def expand(source, d):
+        repeated = dot(source, spread)
+        for b in range(blocks):
+            one = repeated[b * rows:(b + 1) * rows]
+            parts = [jnp.where(piece_of == j, one, 0.0) for j in range(pieces)]
+            half, at = divmod(b, half_blocks)
+            expanded[d, half * band:(half + 1) * band, at * wide:(at + 1) * wide] = (
+                jnp.concatenate(parts, axis=0).astype(jnp.bfloat16)
+            )
+
+    expand(hs_own[...], 0)
+    total[...] = jnp.zeros_like(total)
+    head_width = query_ref.shape[2]
+    position = jnp.concatenate(
+        [jnp.full((1, head_width), lengths_ref[r], jnp.int32) for r in range(rows)], axis=0
+    ).astype(jnp.float32)
+    lane = lax.broadcasted_iota(jnp.int32, (rows, head_width), 1) & (head_width // 2 - 1)
+    frequency = jnp.exp(lane.astype(jnp.float32) * (-2.0 * math.log(500000.0) / head_width))
+    cosine, sine = jnp.cos(position * frequency), jnp.sin(position * frequency)
     chunk = min(1024, half_depth)
 
     def accumulate(d):
@@ -250,6 +247,9 @@
     low_copies = [
         remote(low_own, low_rx.at[d - 1], {"tensor": t_at(d)}) for d in range(1, tensor_size)
     ]
+    t_copies = [
+        remote(hs_own, hs_t.at[d - 1], {"tensor": t_at(d)}) for d in range(1, tensor_size)
+    ]
 
     for part in range(2):
         for load in cache_loads[2 * part:2 * part + 2]:
@@ -352,7 +352,7 @@
     return pl.pallas_call(
         functools.partial(project_kernel, tensor_size, replica_size, pieces),
         out_shape=jax.ShapeDtypeStruct(
-            (rows, queries.shape[1] * queries.shape[2]), jnp.float32
+            (rows, queries.shape[1] * queries.shape[2]), jnp.bfloat16
         ),
         in_specs=[vmem, vmem, smem, smem, hbm, hbm, hbm, hbm, hbm],
         out_specs=vmem,
@@ -389,7 +389,7 @@
             bytes_accessed=2 * (weight.size + down.size + up.size),
             transcendentals=0,
         ),
-    )(hidden, queries, lengths, ids, keys, values, weight, down, up).astype(jnp.bfloat16)
+    )(hidden, queries, lengths, ids, keys, values, weight, down, up)
 
 
 def solution(mesh):

time: 20.1 us -> 20 us (level)
  other arithmetic: 1.46 us -> 0 us
  local copies, waits for them, and re-layouts: 0 us -> 1.38 us
    convert_element_type x1 -> x0, other arithmetic: 1.46 us -> none  [project(): return pl.pallas_call(functools.partial(project_kernel, tensor_size, repl...]
    unnamed x0 -> x1, local copies, waits for them, and re-layouts: none -> 1.38 us
where the time goes in v4:
time: 20 us; the launch traced here: 19.8 us
  Pallas kernels  18.4 us (92%)
  local copies, waits for them, and re-layouts  1.38 us (7%)
    pallas_call x1, Pallas kernels, project(): pl.pallas_call(functools.partial(project_kernel, tensor_size, replica_siz...  18.4 us
    unnamed x1, local copies, waits for them, and re-layouts  1.38 us

profile of v4, /device:TPU:0, one launch (start us, length us, event | category | flops | bytes accessed | tf_op | source)
XLA Modules:
  0.0 19.8 jit_solution(3990280520600185666)
XLA Ops:
  0.0 18.4 %shard_map.91 = bf16[8,2048]{1,0:T(8,128)(2,1)} custom-call(bf16[8,2048]{1,0:T(8,128)(2,1)} %h_ref.1, bf16[8,16,128]{2,1,0:T(8,128)(2,1)} %query_ref.1, s32[8]{0:T(128)} %lengths_ref.1, s32[8]{0:T(128)} %index_ref.1, bf16[8,2,1024,128]{3,2,1,0:T(8,128)(2,1)} %key_hbm.1, bf16[8,2,1024,128]{3,2,1,0:T(8,128)(2,1)} %value_hbm.1, bf16[32768,128]{1,0:T(8,128)(2,1)} %bitcast.9, ...), custom_call_target="tpu_custom_call" | custom-call | flops 67108864 | bytes 10747904 | tf_op jit(solution)/shard_map/pallas_call | solution.py:352
  18.4 1.4 %copy.12 = bf16[8,2048]{1,0:T(8,128)(2,1)} copy(bf16[8,2048]{1,0:T(8,128)(2,1)} %shard_map.91) | data formatting | bytes 65536

commit v5 on v4

--- a/solution.py
+++ b/solution.py
@@ -251,11 +251,13 @@
         remote(hs_own, hs_t.at[d - 1], {"tensor": t_at(d)}) for d in range(1, tensor_size)
     ]
 
-    for part in range(2):
+    def attend_half(part):
         for load in cache_loads[2 * part:2 * part + 2]:
             load.wait()
         for r in range(part * row_half, (part + 1) * row_half):
             attend(r)
+
+    attend_half(0)
 
     loads[1].wait()
     for copy in low_copies:
@@ -295,6 +297,7 @@
         for d in range(1, replica_size)
     ]
 
+    attend_half(1)
     for d in range(1, tensor_size):
         t_copies[d - 1].wait_recv()
         expand(hs_t[d - 1], d)

time: 20 us -> 21.6 us (1.080)
  Pallas kernels: 18.4 us -> 19.9 us
    pallas_call x1, Pallas kernels: 18.4 us -> 19.9 us  [project(): pl.pallas_call(functools.partial(project_kernel, tensor_size, replica_siz...]
where the time goes in v5:
time: 21.6 us; the launch traced here: 21.3 us
  Pallas kernels  19.9 us (92%)
  local copies, waits for them, and re-layouts  1.38 us (6%)
    pallas_call x1, Pallas kernels, project(): pl.pallas_call(functools.partial(project_kernel, tensor_size, replica_siz...  19.9 us
    unnamed x1, local copies, waits for them, and re-layouts  1.38 us

profile of v5, /device:TPU:0, one launch (start us, length us, event | category | flops | bytes accessed | tf_op | source)
XLA Modules:
  0.0 21.3 jit_solution(15977371226898982)
XLA Ops:
  0.0 19.9 %shard_map.91 = bf16[8,2048]{1,0:T(8,128)(2,1)} custom-call(bf16[8,2048]{1,0:T(8,128)(2,1)} %h_ref.1, bf16[8,16,128]{2,1,0:T(8,128)(2,1)} %query_ref.1, s32[8]{0:T(128)} %lengths_ref.1, s32[8]{0:T(128)} %index_ref.1, bf16[8,2,1024,128]{3,2,1,0:T(8,128)(2,1)} %key_hbm.1, bf16[8,2,1024,128]{3,2,1,0:T(8,128)(2,1)} %value_hbm.1, bf16[32768,128]{1,0:T(8,128)(2,1)} %bitcast.9, ...), custom_call_target="tpu_custom_call" | custom-call | flops 67108864 | bytes 10747904 | tf_op jit(solution)/shard_map/pallas_call | solution.py:355
  19.9 1.4 %copy.12 = bf16[8,2048]{1,0:T(8,128)(2,1)} copy(bf16[8,2048]{1,0:T(8,128)(2,1)} %shard_map.91) | data formatting | bytes 65536
